TPU v7x, 256 devices: a whole 4x4x8 slice. The times are simulated.
256 devices in a mesh: region: 8 (over x, core), dev: 32 (over z, y).
Axes of the slice: x: 4, y: 4, z: 8, core: 2. Of those that a mesh axis runs over, the one named last changes fastest.
Arguments:
- features: bfloat16 [64, 64, 256, 128], P(None, 'region', 'dev'), may hold values from -6 to 6
- occupancy: int32 [8, 32, 16], replicated, may hold values from 0 to 1
- weight_one: bfloat16 [64, 64, 3, 3, 3], replicated, may hold values from -0.15625 to 0.15625
- bias_one: float32 [64], replicated, may hold values from -3 to 3
- weight_two: bfloat16 [64, 64, 3, 3, 3], replicated, may hold values from -0.15625 to 0.15625
- bias_two: float32 [64], replicated, may hold values from -3 to 3
- weight_down: bfloat16 [64, 64, 2, 2, 2], replicated, may hold values from -0.25 to 0.25
- bias_down: float32 [64], replicated, may hold values from -3 to 3
Outputs:
- skip_maps: bfloat16 [64, 64, 256, 128], P(None, 'region', 'dev')
- down_maps: bfloat16 [64, 32, 8192], P(None, 'region', 'dev')
All inputs are finite; a program needn't handle non-finite values.
Results may differ from a plain program's by a relative error of at most 0.0047.
Values may be sent and summed in bfloat16 or wider, within the bound.
A program may use at most 128 MiB of HBM per device.

v0:
```python
import functools

import jax
import jax.numpy as jnp
from jax import lax
from jax.experimental import pallas as pl
from jax.experimental.pallas import tpu as pltpu
from jax.sharding import PartitionSpec as P

MESH = pl.DeviceIdType.MESH
WAYS = ((0, 1), (0, -1), (1, 0), (-1, 0), (1, 1), (1, -1), (-1, 1), (-1, -1))
E = 8
C = 64
Z = 128
TAPS = 9


def source_span(step):
    return pl.ds(1, E) if step == 0 else pl.ds(E if step > 0 else 1, 1)


def landing_span(step):
    return pl.ds(1, E) if step == 0 else pl.ds(0 if step > 0 else E + 1, 1)


def column(row):
    spread = jnp.broadcast_to(row, (C, C))
    on_diagonal = lax.broadcasted_iota(jnp.int32, (C, C), 0) == lax.broadcasted_iota(jnp.int32, (C, C), 1)
    return jnp.sum(jnp.where(on_diagonal, spread, 0.0), axis=1, keepdims=True)


def prepare_weight(held, ready):
    for c in range(3):
        rows = pl.ds(c * C, C)
        for pair in range(TAPS // 2):
            both = jnp.concatenate([held[(2 * pair) * 3 + c], held[(2 * pair + 1) * 3 + c]], axis=1)
            ready[rows, pl.ds(pair * 2 * C, 2 * C)] = both
        ready[rows, pl.ds((TAPS - 1) * C, C)] = held[(TAPS - 1) * 3 + c]


def conv_pair(src, ready, bias, mask, spots, put):
    stacked = []
    for a in range(3):
        for b in range(3):
            stacked.append(jnp.concatenate([src[x + a - 1, y + b - 1] for x, y in spots], axis=1))
    sums = jnp.dot(ready[...], jnp.concatenate(stacked, axis=0), preferred_element_type=jnp.float32)
    lane = lax.broadcasted_iota(jnp.int32, (C, Z), 1)
    for half, (x, y) in enumerate(spots):
        part = sums[:, half * Z : (half + 1) * Z]
        before = jnp.where(lane == 0, 0.0, pltpu.roll(part[:C], 1, 1))
        after = jnp.where(lane == Z - 1, 0.0, pltpu.roll(part[2 * C :], Z - 1, 1))
        value = part[C : 2 * C] + before + after + bias
        put(x, y, (jnp.maximum(value, 0.0) * mask).astype(jnp.bfloat16))


def interior(step, pair):
    def body(i, carry):
        for y in range(2, E, 2):
            pair(((i, y), (i, y + 1)))
        return carry

    lax.fori_loop(2, E, body, 0)


def x_rows(pair):
    def body(i, carry):
        x = 1 + i * (E - 1)
        for y in range(2, E, 2):
            pair(((x, y), (x, y + 1)))
        return carry

    lax.fori_loop(0, 2, body, 0)


def y_columns(pair):
    def body(i, carry):
        x = 1 + 2 * i
        for y in (1, E):
            pair(((x, y), (x + 1, y)))
        return carry

    lax.fori_loop(0, E // 2, body, 0)


def remote_kernel(
    shape, feat_hbm, occ_ref, w1_hbm, b1_ref, w2_hbm, b2_ref, second_ref,
    feat, stage, first_in, second_in, w_held, w1, w2, mask_ref, bias_ref, copy_sem, send_sem, recv_sem,
):
    n_region, n_dev = shape
    region, dev = lax.axis_index("region"), lax.axis_index("dev")
    loads = [
        pltpu.make_async_copy(feat_hbm, feat, copy_sem.at[0]),
        pltpu.make_async_copy(w1_hbm, w_held.at[0], copy_sem.at[1]),
        pltpu.make_async_copy(w2_hbm, w_held.at[1], copy_sem.at[2]),
    ]
    for load in loads:
        load.start()

    def there(dr, dd):
        r, d = region + dr, dev + dd
        return (r >= 0) & (r < n_region) & (d >= 0) & (d < n_dev)

    barrier = pltpu.get_barrier_semaphore()
    count = 0
    for dr, dd in WAYS:
        here = there(dr, dd)
        count = count + here.astype(jnp.int32)

        @pl.when(here)
        def _():
            pl.semaphore_signal(barrier, inc=1, device_id=(region + dr, dev + dd), device_id_type=MESH)

    def transfers(buf, turn):
        made = []
        for k, (dr, dd) in enumerate(WAYS):
            copy = pltpu.make_async_remote_copy(
                src_ref=buf.at[source_span(dr), source_span(dd)],
                dst_ref=buf.at[landing_span(dr), landing_span(dd)],
                send_sem=send_sem.at[turn, k],
                recv_sem=recv_sem.at[turn, k],
                device_id=(region + dr, dev + dd),
                device_id_type=MESH,
            )
            made.append((copy, there(dr, dd), there(-dr, -dd)))
        return made

    def start(made):
        for copy, goes, _ in made:
            pl.when(goes)(copy.start)

    def arrived(made):
        for copy, _, comes in made:
            pl.when(comes)(copy.wait_recv)

    def sent(made):
        for copy, goes, _ in made:
            pl.when(goes)(copy.wait_send)

    for dr, dd in WAYS:

        @pl.when(jnp.logical_not(there(-dr, -dd)))
        def _():
            nx, ny = (E if dr == 0 else 1), (E if dd == 0 else 1)
            for buf in (first_in, second_in):
                buf[landing_span(dr), landing_span(dd)] = jnp.zeros((nx, ny, C, Z), jnp.bfloat16)

    mine = occ_ref[region].astype(jnp.float32)
    bricks, devs = mine.shape
    picked = jnp.where(lax.broadcasted_iota(jnp.int32, (bricks, devs), 1) == dev, mine, 0.0)
    level = jnp.sum(picked, axis=1, keepdims=True)
    brick = lax.broadcasted_iota(jnp.int32, (bricks, Z), 0)
    voxel = lax.broadcasted_iota(jnp.int32, (bricks, Z), 1)
    span = Z // bricks
    inside = (voxel >= brick * span) & (voxel < (brick + 1) * span)
    mask_ref[...] = jnp.sum(jnp.where(inside, level, 0.0), axis=0, keepdims=True)
    bias_ref[0] = jnp.broadcast_to(column(b1_ref[...]), (C, Z))
    bias_ref[1] = jnp.broadcast_to(column(b2_ref[...]), (C, Z))
    mask = mask_ref[...]

    loads[0].wait()
    rows = feat.shape[0]
    chunk = 256

    def widen(i, carry):
        at = pl.ds(pl.multiple_of(i * chunk, chunk), chunk)
        stage[at, :] = jnp.where(mask > 0, feat[at, :].astype(jnp.float32), 0.0)
        return carry

    lax.fori_loop(0, rows // chunk, widen, 0)

    def regroup(x, carry):
        for y in range(E):
            first_in[x + 1, y + 1] = stage[pl.ds(x * E + y, C, stride=E * E), :].astype(jnp.bfloat16)
        return carry

    lax.fori_loop(0, E, regroup, 0)

    pl.semaphore_wait(barrier, count)
    one = transfers(first_in, 0)
    start(one)
    loads[1].wait()
    prepare_weight(w_held.at[0], w1)
    loads[2].wait()
    prepare_weight(w_held.at[1], w2)

    def put_first(x, y, value):
        second_in[x, y] = value

    def put_second(x, y, value):
        second_ref[x - 1, y - 1] = value

    def pair_one(spots):
        conv_pair(first_in, w1, bias_ref[0], mask, spots, put_first)

    def pair_two(spots):
        conv_pair(second_in, w2, bias_ref[1], mask, spots, put_second)

    interior(0, pair_one)
    arrived(one[2:4])
    x_rows(pair_one)
    arrived(one[:2])
    arrived(one[4:])
    y_columns(pair_one)
    two = transfers(second_in, 1)
    start(two)
    interior(1, pair_two)
    arrived(two[2:4])
    x_rows(pair_two)
    arrived(two[:2])
    arrived(two[4:])
    y_columns(pair_two)
    sent(one)
    sent(two)


def local_kernel(second_ref, wd_ref, bd_ref, skip_ref, down_ref, stage, wide, wd, narrow):
    def spread(x, carry):
        for y in range(E):
            stage[pl.ds(x * E + y, C, stride=E * E), :] = second_ref[x, y].astype(jnp.float32)
        return carry

    lax.fori_loop(0, E, spread, 0)
    rows = stage.shape[0]
    chunk = 256

    def pack(i, carry):
        at = pl.ds(pl.multiple_of(i * chunk, chunk), chunk)
        skip_ref[at, :] = stage[at, :].astype(jnp.bfloat16)
        return carry

    lax.fori_loop(0, rows // chunk, pack, 0)

    wide[...] = wd_ref[...].astype(jnp.float32)
    for c in range(2):
        for a in range(2):
            both = [wide[pl.ds(a * 4 + b * 2 + c, C, stride=8), :].astype(jnp.bfloat16) for b in range(2)]
            wd[pl.ds(c * C, C), pl.ds(a * 2 * C, 2 * C)] = jnp.concatenate(both, axis=1)
    lane_in = lax.broadcasted_iota(jnp.int32, (2 * Z, Z), 0)
    lane_out = lax.broadcasted_iota(jnp.int32, (2 * Z, Z), 1)
    keep = jnp.where(lane_in == 2 * lane_out, 1.0, 0.0).astype(jnp.bfloat16)
    bias = jnp.broadcast_to(column(bd_ref[...]), (C, 2 * Z))
    half = E // 2

    def lower(x, carry):
        for y in range(0, E, 4):
            stacked = [
                jnp.concatenate([second_ref[2 * x + a, y + 2 * k + b] for k in range(2)], axis=1)
                for a in range(2)
                for b in range(2)
            ]
            sums = jnp.dot(wd[...], jnp.concatenate(stacked, axis=0), preferred_element_type=jnp.float32)
            moved = jnp.concatenate([pltpu.roll(sums[C:, k * Z : (k + 1) * Z], Z - 1, 1) for k in range(2)], axis=1)
            value = jnp.maximum(sums[:C] + moved + bias, 0.0).astype(jnp.bfloat16)
            narrow[y // 4, pl.ds(x, C, stride=half), :] = jnp.dot(value, keep, preferred_element_type=jnp.float32)
        return carry

    lax.fori_loop(0, half, lower, 0)
    for k in range(2):
        down_ref[:, :, pl.ds(k * Z, Z)] = narrow[k].reshape(C, half, Z).astype(jnp.bfloat16)


def on_device(shape, features, occupancy, weight_one, bias_one, weight_two, bias_two, weight_down, bias_down):
    bf16, f32 = jnp.bfloat16, jnp.float32
    any_space = pl.BlockSpec(memory_space=pl.ANY)
    vmem = pl.BlockSpec(memory_space=pltpu.VMEM)
    rows = C * E * E
    held = [w.transpose(2, 3, 4, 0, 1).reshape(27, C, C) for w in (weight_one, weight_two)]
    second = pl.pallas_call(
        functools.partial(remote_kernel, shape),
        out_shape=jax.ShapeDtypeStruct((E, E, C, Z), bf16),
        in_specs=[any_space, vmem, any_space, vmem, any_space, vmem],
        out_specs=vmem,
        scratch_shapes=[
            pltpu.VMEM((rows, Z), bf16),
            pltpu.VMEM((rows, Z), f32),
            pltpu.VMEM((E + 2, E + 2, C, Z), bf16),
            pltpu.VMEM((E + 2, E + 2, C, Z), bf16),
            pltpu.VMEM((2, 27, C, C), bf16),
            pltpu.VMEM((3 * C, TAPS * C), bf16),
            pltpu.VMEM((3 * C, TAPS * C), bf16),
            pltpu.VMEM((1, Z), f32),
            pltpu.VMEM((2, C, Z), f32),
            pltpu.SemaphoreType.DMA((3,)),
            pltpu.SemaphoreType.DMA((2, len(WAYS))),
            pltpu.SemaphoreType.DMA((2, len(WAYS))),
        ],
        compiler_params=pltpu.CompilerParams(
            collective_id=0, has_side_effects=True, vmem_limit_bytes=32 * 1024 * 1024
        ),
        name="halo_convs",
    )(
        features.reshape(rows, Z),
        occupancy.transpose(0, 2, 1),
        held[0],
        bias_one.reshape(1, C),
        held[1],
        bias_two.reshape(1, C),
    )
    skip, down = pl.pallas_call(
        local_kernel,
        out_shape=(
            jax.ShapeDtypeStruct((rows, Z), bf16),
            jax.ShapeDtypeStruct((C, E // 2, 2 * Z), bf16),
        ),
        in_specs=[vmem] * 3,
        out_specs=(vmem, vmem),
        scratch_shapes=[
            pltpu.VMEM((rows, Z), f32),
            pltpu.VMEM((8 * C, C), f32),
            pltpu.VMEM((2 * C, 4 * C), bf16),
            pltpu.VMEM((2, C * E // 2, Z), f32),
        ],
        compiler_params=pltpu.CompilerParams(vmem_limit_bytes=32 * 1024 * 1024),
        name="skip_and_down",
    )(second, weight_down.transpose(0, 2, 3, 4, 1).reshape(8 * C, C), bias_down.reshape(1, C))
    return skip.reshape(C, E, E, Z), down


def solution(mesh):
    return jax.shard_map(
        functools.partial(on_device, (mesh.shape["region"], mesh.shape["dev"])),
        mesh=mesh,
        in_specs=(P(None, "region", "dev", None), P(), P(), P(), P(), P(), P(), P()),
        out_specs=(P(None, "region", "dev", None), P(None, "region", "dev")),
        check_vma=False,
    )
```

profile of v0, /device:TPU:121, one launch (start us, length us, event | category | flops | bytes accessed | tf_op | source)
XLA Modules:
  0.0 34.3 jit_solution(13593903951379244401)
XLA Ops:
  0.6 0.0 copy-start.6
  0.6 0.0 copy-start.7
  0.7 0.6 %copy-done.6 = f32[64]{0:T(128)S(1)} copy-done((f32[64]{0:T(128)S(1)}, f32[64]{0:T(128)}, u32[]{:S(2)}) %copy-start.6) | copy-done | bytes 280
  1.3 0.0 copy-done.7
  1.3 0.0 copy-start
  1.3 1.2 %copy-done = bf16[64,8,8,128]{3,2,1,0:T(8,128)(2,1)S(1)} copy-done((bf16[64,8,8,128]{3,2,1,0:T(8,128)(2,1)S(1)}, bf16[64,8,8,128]{3,2,1,0:T(8,128)(2,1)}, u32[]{:S(2)}) %copy-start) | copy-done | bytes 1048600
  2.5 0.0 copy-start.1
  2.5 1.0 %copy-done.1 = bf16[64,64,3,3,3]{1,0,4,3,2:T(8,128)(2,1)S(1)} copy-done((bf16[64,64,3,3,3]{1,0,4,3,2:T(8,128)(2,1)S(1)}, bf16[64,64,3,3,3]{1,0,4,3,2:T(8,128)(2,1)}, u32[]{:S(2)}) %copy-start.1) | copy-done | bytes 221208
  3.5 0.0 copy-start.2
  3.5 1.0 %copy-done.2 = bf16[64,64,3,3,3]{1,0,4,3,2:T(8,128)(2,1)S(1)} copy-done((bf16[64,64,3,3,3]{1,0,4,3,2:T(8,128)(2,1)S(1)}, bf16[64,64,3,3,3]{1,0,4,3,2:T(8,128)(2,1)}, u32[]{:S(2)}) %copy-start.2) | copy-done | bytes 221208
  4.6 0.0 copy-start.4
  4.6 0.8 %copy-done.4 = s32[8,32,16]{1,2,0:T(8,128)S(1)} copy-done((s32[8,32,16]{1,2,0:T(8,128)S(1)}, s32[8,32,16]{1,2,0:T(8,128)}, u32[]{:S(2)}) %copy-start.4) | copy-done | bytes 16408
  5.4 0.0 copy-start.3
  5.4 0.0 copy-start.5
  5.4 23.3 %halo_convs.1.second_ref = bf16[8,8,64,128]{3,2,1,0:T(8,128)(2,1)S(1)} custom-call(bf16[4096,128]{1,0:T(8,128)(2,1)S(1)} %bitcast.15, s32[8,16,32]{2,1,0:T(8,128)S(1)} %bitcast.19, bf16[27,64,64]{2,1,0:T(8,128)(2,1)S(1)} %bitcast.16, f32[1,64]{1,0:T(1,128)S(1)} %bitcast.21, bf16[27,64,64]{2,1,0:T(8,128)(2,1)S(1)} %bitcast.17, f32[1,64]{1,0:T(1,128)S(1)} %bitcast.22), custom_call_target="tpu_custom_call" | custom-call | tf_op jit(solution)/shard_map/halo_convs/pallas_call | solution.py:268
  28.8 0.0 copy-done.3
  28.8 0.0 copy-done.5
  28.8 5.5 %skip_and_down.1 = (bf16[4096,128]{1,0:T(8,128)(2,1)}, bf16[64,4,256]{2,1,0:T(4,128)(2,1)}) custom-call(bf16[8,8,64,128]{3,2,1,0:T(8,128)(2,1)S(1)} %halo_convs.1.second_ref, bf16[512,64]{1,0:T(8,128)(2,1)S(1)} %bitcast.18, f32[1,64]{1,0:T(1,128)S(1)} %bitcast.20), custom_call_target="tpu_custom_call" | custom-call | tf_op jit(solution)/shard_map/skip_and_down/pallas_call | solution.py:299
Async XLA Ops:
  0.6 0.7 %copy-start.6 = (f32[64]{0:T(128)S(1)}, f32[64]{0:T(128)}, u32[]{:S(2)}) copy-start(f32[64]{0:T(128)} %param.11) | copy-start | bytes 772
  0.6 0.7 %copy-start.7 = (f32[64]{0:T(128)S(1)}, f32[64]{0:T(128)}, u32[]{:S(2)}) copy-start(f32[64]{0:T(128)} %param.13) | copy-start | bytes 772
  1.3 1.2 %copy-start = (bf16[64,8,8,128]{3,2,1,0:T(8,128)(2,1)S(1)}, bf16[64,8,8,128]{3,2,1,0:T(8,128)(2,1)}, u32[]{:S(2)}) copy-start(bf16[64,8,8,128]{3,2,1,0:T(8,128)(2,1)} %param.8) | copy-start | bytes 3145732
  2.5 1.0 %copy-start.1 = (bf16[64,64,3,3,3]{1,0,4,3,2:T(8,128)(2,1)S(1)}, bf16[64,64,3,3,3]{1,0,4,3,2:T(8,128)(2,1)}, u32[]{:S(2)}) copy-start(bf16[64,64,3,3,3]{1,0,4,3,2:T(8,128)(2,1)} %param.10) | copy-start | bytes 663556
  3.5 1.0 %copy-start.2 = (bf16[64,64,3,3,3]{1,0,4,3,2:T(8,128)(2,1)S(1)}, bf16[64,64,3,3,3]{1,0,4,3,2:T(8,128)(2,1)}, u32[]{:S(2)}) copy-start(bf16[64,64,3,3,3]{1,0,4,3,2:T(8,128)(2,1)} %param.12) | copy-start | bytes 663556
  4.6 0.8 %copy-start.4 = (s32[8,32,16]{1,2,0:T(8,128)S(1)}, s32[8,32,16]{1,2,0:T(8,128)}, u32[]{:S(2)}) copy-start(s32[8,32,16]{1,2,0:T(8,128)} %param.9) | copy-start | bytes 49156
  5.4 23.4 %copy-start.3 = (bf16[64,64,2,2,2]{1,4,3,2,0:T(2,128)(2,1)S(1)}, bf16[64,64,2,2,2]{1,4,3,2,0:T(2,128)(2,1)}, u32[]{:S(2)}) copy-start(bf16[64,64,2,2,2]{1,4,3,2,0:T(2,128)(2,1)} %param.14) | copy-start | bytes 196612
  5.4 23.4 %copy-start.5 = (f32[64]{0:T(128)S(1)}, f32[64]{0:T(128)}, u32[]{:S(2)}) copy-start(f32[64]{0:T(128)} %param.15) | copy-start | bytes 772
where the time goes:
time: 34.5 us; the launch traced here: 34.3 us
  Pallas kernels  28.9 us (84%)
  local copies, waits for them, and re-layouts  4.75 us (14%)
  between operations  0.68 us (2%)
    pallas_call x1, Pallas kernels, on_device(): pl.pallas_call(functools.partial(remote_kernel, shape), out_shape=jax.Sha...  23.3 us
    pallas_call x1, Pallas kernels, on_device(): pl.pallas_call(local_kernel, out_shape=(jax.ShapeDtypeStruct((rows, Z), b...  5.51 us
    unnamed x16, local copies, waits for them, and re-layouts  4.75 us

commit v1 on v0

--- a/solution.py
+++ b/solution.py
@@ -53,38 +53,27 @@
         put(x, y, (jnp.maximum(value, 0.0) * mask).astype(jnp.bfloat16))
 
 
-def interior(step, pair):
-    def body(i, carry):
-        for y in range(2, E, 2):
-            pair(((i, y), (i, y + 1)))
-        return carry
-
-    lax.fori_loop(2, E, body, 0)
-
-
-def x_rows(pair):
-    def body(i, carry):
-        x = 1 + i * (E - 1)
+def interior(pair):
+    for x in range(2, E):
         for y in range(2, E, 2):
             pair(((x, y), (x, y + 1)))
-        return carry
-
-    lax.fori_loop(0, 2, body, 0)
+
+
+def x_rows(pair):
+    for x in (1, E):
+        for y in range(2, E, 2):
+            pair(((x, y), (x, y + 1)))
 
 
 def y_columns(pair):
-    def body(i, carry):
-        x = 1 + 2 * i
+    for x in range(1, E, 2):
         for y in (1, E):
             pair(((x, y), (x + 1, y)))
-        return carry
-
-    lax.fori_loop(0, E // 2, body, 0)
 
 
 def remote_kernel(
-    shape, feat_hbm, occ_ref, w1_hbm, b1_ref, w2_hbm, b2_ref, second_ref,
-    feat, stage, first_in, second_in, w_held, w1, w2, mask_ref, bias_ref, copy_sem, send_sem, recv_sem,
+    shape, feat_hbm, occ_hbm, w1_hbm, b1_hbm, w2_hbm, b2_hbm, second_ref,
+    feat, occ_ref, b_held, first_in, second_in, w_held, w1, w2, mask_ref, bias_ref, copy_sem, send_sem, recv_sem,
 ):
     n_region, n_dev = shape
     region, dev = lax.axis_index("region"), lax.axis_index("dev")
@@ -92,6 +81,9 @@
         pltpu.make_async_copy(feat_hbm, feat, copy_sem.at[0]),
         pltpu.make_async_copy(w1_hbm, w_held.at[0], copy_sem.at[1]),
         pltpu.make_async_copy(w2_hbm, w_held.at[1], copy_sem.at[2]),
+        pltpu.make_async_copy(occ_hbm, occ_ref, copy_sem.at[3]),
+        pltpu.make_async_copy(b1_hbm, b_held.at[0], copy_sem.at[4]),
+        pltpu.make_async_copy(b2_hbm, b_held.at[1], copy_sem.at[5]),
     ]
     for load in loads:
         load.start()
@@ -144,6 +136,7 @@
             for buf in (first_in, second_in):
                 buf[landing_span(dr), landing_span(dd)] = jnp.zeros((nx, ny, C, Z), jnp.bfloat16)
 
+    loads[3].wait()
     mine = occ_ref[region].astype(jnp.float32)
     bricks, devs = mine.shape
     picked = jnp.where(lax.broadcasted_iota(jnp.int32, (bricks, devs), 1) == dev, mine, 0.0)
@@ -153,27 +146,15 @@
     span = Z // bricks
     inside = (voxel >= brick * span) & (voxel < (brick + 1) * span)
     mask_ref[...] = jnp.sum(jnp.where(inside, level, 0.0), axis=0, keepdims=True)
-    bias_ref[0] = jnp.broadcast_to(column(b1_ref[...]), (C, Z))
-    bias_ref[1] = jnp.broadcast_to(column(b2_ref[...]), (C, Z))
     mask = mask_ref[...]
 
     loads[0].wait()
-    rows = feat.shape[0]
-    chunk = 256
-
-    def widen(i, carry):
-        at = pl.ds(pl.multiple_of(i * chunk, chunk), chunk)
-        stage[at, :] = jnp.where(mask > 0, feat[at, :].astype(jnp.float32), 0.0)
-        return carry
-
-    lax.fori_loop(0, rows // chunk, widen, 0)
-
-    def regroup(x, carry):
-        for y in range(E):
-            first_in[x + 1, y + 1] = stage[pl.ds(x * E + y, C, stride=E * E), :].astype(jnp.bfloat16)
-        return carry
-
-    lax.fori_loop(0, E, regroup, 0)
+    for x in range(0, E, 2):
+        slab = jnp.concatenate([feat[pl.ds(c * E * E + x * E, 2 * E), :] for c in range(C)], axis=0)
+        blocks = jnp.swapaxes(slab.reshape(C, 2 * E, Z), 0, 1)
+        blocks = jnp.where(mask[None] > 0, blocks, jnp.zeros_like(blocks))
+        for k in range(2):
+            first_in[x + k + 1, pl.ds(1, E)] = blocks[k * E : (k + 1) * E]
 
     pl.semaphore_wait(barrier, count)
     one = transfers(first_in, 0)
@@ -182,6 +163,9 @@
     prepare_weight(w_held.at[0], w1)
     loads[2].wait()
     prepare_weight(w_held.at[1], w2)
+    for k in range(2):
+        loads[4 + k].wait()
+        bias_ref[k] = jnp.broadcast_to(column(b_held[k]), (C, Z))
 
     def put_first(x, y, value):
         second_in[x, y] = value
@@ -195,7 +179,7 @@
     def pair_two(spots):
         conv_pair(second_in, w2, bias_ref[1], mask, spots, put_second)
 
-    interior(0, pair_one)
+    interior(pair_one)
     arrived(one[2:4])
     x_rows(pair_one)
     arrived(one[:2])
@@ -203,7 +187,7 @@
     y_columns(pair_one)
     two = transfers(second_in, 1)
     start(two)
-    interior(1, pair_two)
+    interior(pair_two)
     arrived(two[2:4])
     x_rows(pair_two)
     arrived(two[:2])
@@ -213,22 +197,11 @@
     sent(two)
 
 
-def local_kernel(second_ref, wd_ref, bd_ref, skip_ref, down_ref, stage, wide, wd, narrow):
-    def spread(x, carry):
-        for y in range(E):
-            stage[pl.ds(x * E + y, C, stride=E * E), :] = second_ref[x, y].astype(jnp.float32)
-        return carry
-
-    lax.fori_loop(0, E, spread, 0)
-    rows = stage.shape[0]
-    chunk = 256
-
-    def pack(i, carry):
-        at = pl.ds(pl.multiple_of(i * chunk, chunk), chunk)
-        skip_ref[at, :] = stage[at, :].astype(jnp.bfloat16)
-        return carry
-
-    lax.fori_loop(0, rows // chunk, pack, 0)
+def local_kernel(second_ref, wd_ref, bd_ref, skip_ref, down_ref, wide, wd, narrow):
+    for x in range(0, E, 2):
+        blocks = jnp.swapaxes(jnp.concatenate([second_ref[x], second_ref[x + 1]], axis=0), 0, 1)
+        for o in range(C):
+            skip_ref[pl.ds(o * E * E + x * E, 2 * E), :] = blocks[o]
 
     wide[...] = wd_ref[...].astype(jnp.float32)
     for c in range(2):
@@ -241,7 +214,7 @@
     bias = jnp.broadcast_to(column(bd_ref[...]), (C, 2 * Z))
     half = E // 2
 
-    def lower(x, carry):
+    for x in range(half):
         for y in range(0, E, 4):
             stacked = [
                 jnp.concatenate([second_ref[2 * x + a, y + 2 * k + b] for k in range(2)], axis=1)
@@ -252,27 +225,25 @@
             moved = jnp.concatenate([pltpu.roll(sums[C:, k * Z : (k + 1) * Z], Z - 1, 1) for k in range(2)], axis=1)
             value = jnp.maximum(sums[:C] + moved + bias, 0.0).astype(jnp.bfloat16)
             narrow[y // 4, pl.ds(x, C, stride=half), :] = jnp.dot(value, keep, preferred_element_type=jnp.float32)
-        return carry
-
-    lax.fori_loop(0, half, lower, 0)
     for k in range(2):
         down_ref[:, :, pl.ds(k * Z, Z)] = narrow[k].reshape(C, half, Z).astype(jnp.bfloat16)
 
 
 def on_device(shape, features, occupancy, weight_one, bias_one, weight_two, bias_two, weight_down, bias_down):
     bf16, f32 = jnp.bfloat16, jnp.float32
-    any_space = pl.BlockSpec(memory_space=pl.ANY)
+    hbm = pl.BlockSpec(memory_space=pltpu.HBM)
     vmem = pl.BlockSpec(memory_space=pltpu.VMEM)
     rows = C * E * E
     held = [w.transpose(2, 3, 4, 0, 1).reshape(27, C, C) for w in (weight_one, weight_two)]
     second = pl.pallas_call(
         functools.partial(remote_kernel, shape),
         out_shape=jax.ShapeDtypeStruct((E, E, C, Z), bf16),
-        in_specs=[any_space, vmem, any_space, vmem, any_space, vmem],
+        in_specs=[hbm] * 6,
         out_specs=vmem,
         scratch_shapes=[
             pltpu.VMEM((rows, Z), bf16),
-            pltpu.VMEM((rows, Z), f32),
+            pltpu.VMEM((shape[0], occupancy.shape[2], shape[1]), jnp.int32),
+            pltpu.VMEM((2, 1, C), f32),
             pltpu.VMEM((E + 2, E + 2, C, Z), bf16),
             pltpu.VMEM((E + 2, E + 2, C, Z), bf16),
             pltpu.VMEM((2, 27, C, C), bf16),
@@ -280,7 +251,7 @@
             pltpu.VMEM((3 * C, TAPS * C), bf16),
             pltpu.VMEM((1, Z), f32),
             pltpu.VMEM((2, C, Z), f32),
-            pltpu.SemaphoreType.DMA((3,)),
+            pltpu.SemaphoreType.DMA((6,)),
             pltpu.SemaphoreType.DMA((2, len(WAYS))),
             pltpu.SemaphoreType.DMA((2, len(WAYS))),
         ],
@@ -305,7 +276,6 @@
         in_specs=[vmem] * 3,
         out_specs=(vmem, vmem),
         scratch_shapes=[
-            pltpu.VMEM((rows, Z), f32),
             pltpu.VMEM((8 * C, C), f32),
             pltpu.VMEM((2 * C, 4 * C), bf16),
             pltpu.VMEM((2, C * E // 2, Z), f32),

time: 34.5 us -> 30.5 us (0.88)
  Pallas kernels: 28.9 us -> 24.8 us
    pallas_call x1, Pallas kernels: 5.51 us -> 2.97 us  [on_device(): pl.pallas_call(local_kernel, out_shape=(jax.ShapeDtypeStruct((rows, Z), b...]
    pallas_call x1, Pallas kernels: 23.3 us -> 21.9 us  [on_device(): pl.pallas_call(functools.partial(remote_kernel, shape), out_shape=jax.Sha...]
where the time goes in v1:
time: 30.5 us; the launch traced here: 30.3 us
  Pallas kernels  24.8 us (81%)
  local copies, waits for them, and re-layouts  4.75 us (16%)
  between operations  0.68 us (2%)
    pallas_call x1, Pallas kernels, on_device(): pl.pallas_call(functools.partial(remote_kernel, shape), out_shape=jax.Sha...  21.9 us
    unnamed x16, local copies, waits for them, and re-layouts  4.75 us
    pallas_call x1, Pallas kernels, on_device(): pl.pallas_call(local_kernel, out_shape=(jax.ShapeDtypeStruct((rows, Z), b...  2.97 us

profile of v1, /device:TPU:121, one launch (start us, length us, event | category | flops | bytes accessed | tf_op | source)
XLA Modules:
  0.0 30.3 jit_solution(14088047778384431156)
XLA Ops:
  0.6 0.0 copy-start.6
  0.6 0.0 copy-start.7
  0.7 0.6 %copy-done.6 = f32[64]{0:T(128)S(1)} copy-done((f32[64]{0:T(128)S(1)}, f32[64]{0:T(128)}, u32[]{:S(2)}) %copy-start.6) | copy-done | bytes 280
  1.3 0.0 copy-done.7
  1.3 0.0 copy-start
  1.3 1.2 %copy-done = bf16[64,8,8,128]{3,2,1,0:T(8,128)(2,1)S(1)} copy-done((bf16[64,8,8,128]{3,2,1,0:T(8,128)(2,1)S(1)}, bf16[64,8,8,128]{3,2,1,0:T(8,128)(2,1)}, u32[]{:S(2)}) %copy-start) | copy-done | bytes 1048600
  2.5 0.0 copy-start.1
  2.5 1.0 %copy-done.1 = bf16[64,64,3,3,3]{1,0,4,3,2:T(8,128)(2,1)S(1)} copy-done((bf16[64,64,3,3,3]{1,0,4,3,2:T(8,128)(2,1)S(1)}, bf16[64,64,3,3,3]{1,0,4,3,2:T(8,128)(2,1)}, u32[]{:S(2)}) %copy-start.1) | copy-done | bytes 221208
  3.5 0.0 copy-start.2
  3.5 1.0 %copy-done.2 = bf16[64,64,3,3,3]{1,0,4,3,2:T(8,128)(2,1)S(1)} copy-done((bf16[64,64,3,3,3]{1,0,4,3,2:T(8,128)(2,1)S(1)}, bf16[64,64,3,3,3]{1,0,4,3,2:T(8,128)(2,1)}, u32[]{:S(2)}) %copy-start.2) | copy-done | bytes 221208
  4.6 0.0 copy-start.4
  4.6 0.8 %copy-done.4 = s32[8,32,16]{1,2,0:T(8,128)S(1)} copy-done((s32[8,32,16]{1,2,0:T(8,128)S(1)}, s32[8,32,16]{1,2,0:T(8,128)}, u32[]{:S(2)}) %copy-start.4) | copy-done | bytes 16408
  5.4 0.0 copy-start.3
  5.4 0.0 copy-start.5
  5.4 21.9 %halo_convs.1.second_ref = bf16[8,8,64,128]{3,2,1,0:T(8,128)(2,1)S(1)} custom-call(bf16[4096,128]{1,0:T(8,128)(2,1)S(1)} %bitcast.15, s32[8,16,32]{2,1,0:T(8,128)S(1)} %bitcast.19, bf16[27,64,64]{2,1,0:T(8,128)(2,1)S(1)} %bitcast.16, f32[1,64]{1,0:T(1,128)S(1)} %bitcast.21, bf16[27,64,64]{2,1,0:T(8,128)(2,1)S(1)} %bitcast.17, f32[1,64]{1,0:T(1,128)S(1)} %bitcast.22), custom_call_target="tpu_custom_call" | custom-call | tf_op jit(solution)/shard_map/halo_convs/pallas_call | solution.py:238
  27.3 0.0 copy-done.3
  27.3 0.0 copy-done.5
  27.3 3.0 %skip_and_down.1 = (bf16[4096,128]{1,0:T(8,128)(2,1)}, bf16[64,4,256]{2,1,0:T(4,128)(2,1)}) custom-call(bf16[8,8,64,128]{3,2,1,0:T(8,128)(2,1)S(1)} %halo_convs.1.second_ref, bf16[512,64]{1,0:T(8,128)(2,1)S(1)} %bitcast.18, f32[1,64]{1,0:T(1,128)S(1)} %bitcast.20), custom_call_target="tpu_custom_call" | custom-call | tf_op jit(solution)/shard_map/skip_and_down/pallas_call | solution.py:270
Async XLA Ops:
  0.6 0.7 %copy-start.6 = (f32[64]{0:T(128)S(1)}, f32[64]{0:T(128)}, u32[]{:S(2)}) copy-start(f32[64]{0:T(128)} %param.11) | copy-start | bytes 772
  0.6 0.7 %copy-start.7 = (f32[64]{0:T(128)S(1)}, f32[64]{0:T(128)}, u32[]{:S(2)}) copy-start(f32[64]{0:T(128)} %param.13) | copy-start | bytes 772
  1.3 1.2 %copy-start = (bf16[64,8,8,128]{3,2,1,0:T(8,128)(2,1)S(1)}, bf16[64,8,8,128]{3,2,1,0:T(8,128)(2,1)}, u32[]{:S(2)}) copy-start(bf16[64,8,8,128]{3,2,1,0:T(8,128)(2,1)} %param.8) | copy-start | bytes 3145732
  2.5 1.0 %copy-start.1 = (bf16[64,64,3,3,3]{1,0,4,3,2:T(8,128)(2,1)S(1)}, bf16[64,64,3,3,3]{1,0,4,3,2:T(8,128)(2,1)}, u32[]{:S(2)}) copy-start(bf16[64,64,3,3,3]{1,0,4,3,2:T(8,128)(2,1)} %param.10) | copy-start | bytes 663556
  3.5 1.0 %copy-start.2 = (bf16[64,64,3,3,3]{1,0,4,3,2:T(8,128)(2,1)S(1)}, bf16[64,64,3,3,3]{1,0,4,3,2:T(8,128)(2,1)}, u32[]{:S(2)}) copy-start(bf16[64,64,3,3,3]{1,0,4,3,2:T(8,128)(2,1)} %param.12) | copy-start | bytes 663556
  4.6 0.8 %copy-start.4 = (s32[8,32,16]{1,2,0:T(8,128)S(1)}, s32[8,32,16]{1,2,0:T(8,128)}, u32[]{:S(2)}) copy-start(s32[8,32,16]{1,2,0:T(8,128)} %param.9) | copy-start | bytes 49156
  5.4 21.9 %copy-start.3 = (bf16[64,64,2,2,2]{1,4,3,2,0:T(2,128)(2,1)S(1)}, bf16[64,64,2,2,2]{1,4,3,2,0:T(2,128)(2,1)}, u32[]{:S(2)}) copy-start(bf16[64,64,2,2,2]{1,4,3,2,0:T(2,128)(2,1)} %param.14) | copy-start | bytes 196612
  5.4 21.9 %copy-start.5 = (f32[64]{0:T(128)S(1)}, f32[64]{0:T(128)}, u32[]{:S(2)}) copy-start(f32[64]{0:T(128)} %param.15) | copy-start | bytes 772

commit v2 on v1

--- a/solution.py
+++ b/solution.py
@@ -260,12 +260,17 @@
         ),
         name="halo_convs",
     )(
-        features.reshape(rows, Z),
-        occupancy.transpose(0, 2, 1),
-        held[0],
-        bias_one.reshape(1, C),
-        held[1],
-        bias_two.reshape(1, C),
+        *(
+            pltpu.with_memory_space_constraint(operand, pltpu.HBM)
+            for operand in (
+                features.reshape(rows, Z),
+                occupancy.transpose(0, 2, 1),
+                held[0],
+                bias_one.reshape(1, C),
+                held[1],
+                bias_two.reshape(1, C),
+            )
+        )
     )
     skip, down = pl.pallas_call(
         local_kernel,

time: 30.5 us -> 25.1 us (0.82)
  local copies, waits for them, and re-layouts: 4.75 us -> 0.01 us
  Pallas kernels: 24.8 us -> 24.3 us
    unnamed x16 -> x4, local copies, waits for them, and re-layouts: 4.75 us -> 0.01 us
    pallas_call x1, Pallas kernels: 21.9 us -> 21.4 us  [on_device(): pl.pallas_call(functools.partial(remote_kernel, shape), out_shape=jax.Sha...]
where the time goes in v2:
time: 25.1 us; the launch traced here: 25 us
  Pallas kernels  24.3 us (97%)
  between operations  0.67 us (3%)
    pallas_call x1, Pallas kernels, on_device(): pl.pallas_call(functools.partial(remote_kernel, shape), out_shape=jax.Sha...  21.4 us
    pallas_call x1, Pallas kernels, on_device(): pl.pallas_call(local_kernel, out_shape=(jax.ShapeDtypeStruct((rows, Z), b...  2.96 us

profile of v2, /device:TPU:121, one launch (start us, length us, event | category | flops | bytes accessed | tf_op | source)
XLA Modules:
  0.0 25.0 jit_solution(499354593393668593)
XLA Ops:
  0.6 0.0 copy-start
  0.6 0.0 copy-start.1
  0.7 21.4 %halo_convs.1.second_ref = bf16[8,8,64,128]{3,2,1,0:T(8,128)(2,1)S(1)} custom-call(bf16[4096,128]{1,0:T(8,128)(2,1)} %bitcast.17, s32[8,16,32]{2,1,0:T(8,128)} %bitcast.20, bf16[27,64,64]{2,1,0:T(8,128)(2,1)} %bitcast.18, f32[1,64]{1,0:T(1,128)} %bitcast.21, bf16[27,64,64]{2,1,0:T(8,128)(2,1)} %bitcast.19, f32[1,64]{1,0:T(1,128)} %bitcast.22), custom_call_target="tpu_custom_call" | custom-call | tf_op jit(solution)/shard_map/halo_convs/pallas_call | solution.py:238
  22.0 0.0 copy-done
  22.0 0.0 copy-done.1
  22.0 3.0 %skip_and_down.1 = (bf16[4096,128]{1,0:T(8,128)(2,1)}, bf16[64,4,256]{2,1,0:T(4,128)(2,1)}) custom-call(bf16[8,8,64,128]{3,2,1,0:T(8,128)(2,1)S(1)} %halo_convs.1.second_ref, bf16[512,64]{1,0:T(8,128)(2,1)S(1)} %bitcast.15, f32[1,64]{1,0:T(1,128)S(1)} %bitcast.16), custom_call_target="tpu_custom_call" | custom-call | tf_op jit(solution)/shard_map/skip_and_down/pallas_call | solution.py:275
Async XLA Ops:
  0.6 21.4 %copy-start = (bf16[64,64,2,2,2]{1,4,3,2,0:T(2,128)(2,1)S(1)}, bf16[64,64,2,2,2]{1,4,3,2,0:T(2,128)(2,1)}, u32[]{:S(2)}) copy-start(bf16[64,64,2,2,2]{1,4,3,2,0:T(2,128)(2,1)} %param.14) | copy-start | bytes 196612
  0.6 21.4 %copy-start.1 = (f32[64]{0:T(128)S(1)}, f32[64]{0:T(128)}, u32[]{:S(2)}) copy-start(f32[64]{0:T(128)} %param.15) | copy-start | bytes 772

commit v3 on v2

v3 whole, which is shorter than its diff:
```python
import functools

import jax
import jax.numpy as jnp
from jax import lax
from jax.experimental import pallas as pl
from jax.experimental.pallas import tpu as pltpu
from jax.sharding import PartitionSpec as P

MESH = pl.DeviceIdType.MESH
CORNERS = ((1, 1), (-1, 1), (1, -1), (-1, -1))
FACES_X = ((1, 0), (-1, 0))
FACES_Y = ((0, 1), (0, -1))
E = 8
H = 2
C = 64
Z = 128
TAPS = 9
CHUNK = 2


def source_span(step):
    return pl.ds(H, E) if step == 0 else pl.ds(E if step > 0 else H, H)


def landing_span(step):
    return pl.ds(H, E) if step == 0 else pl.ds(0 if step > 0 else E + H, H)


def column(row):
    spread = jnp.broadcast_to(row, (C, C))
    on_diagonal = lax.broadcasted_iota(jnp.int32, (C, C), 0) == lax.broadcasted_iota(jnp.int32, (C, C), 1)
    return jnp.sum(jnp.where(on_diagonal, spread, 0.0), axis=1, keepdims=True)


def prepare_weight(held, ready):
    for c in range(3):
        rows = pl.ds(c * C, C)
        for pair in range(TAPS // 2):
            both = jnp.concatenate([held[(2 * pair) * 3 + c], held[(2 * pair + 1) * 3 + c]], axis=1)
            ready[rows, pl.ds(pair * 2 * C, 2 * C)] = both
        ready[rows, pl.ds((TAPS - 1) * C, C)] = held[(TAPS - 1) * 3 + c]


def conv_pair(src, ready, bias, spots, put):
    stacked = []
    for a in range(3):
        for b in range(3):
            stacked.append(jnp.concatenate([src[x + a, y + b] for x, y in spots], axis=1))
    sums = jnp.dot(ready[...], jnp.concatenate(stacked, axis=0), preferred_element_type=jnp.float32)
    lane = lax.broadcasted_iota(jnp.int32, (C, Z), 1)
    for half, (x, y) in enumerate(spots):
        part = sums[:, half * Z : (half + 1) * Z]
        before = jnp.where(lane == 0, 0.0, pltpu.roll(part[:C], 1, 1))
        after = jnp.where(lane == Z - 1, 0.0, pltpu.roll(part[2 * C :], Z - 1, 1))
        put(x, y, jnp.maximum(part[C : 2 * C] + before + after + bias, 0.0))


def remote_kernel(
    shape, feat_hbm, occ_hbm, w1_hbm, b1_hbm, w2_hbm, b2_hbm, wd_hbm, second_ref, wd_ref,
    feat, occ_ref, b_held, grid, first, w_held, w1, w2, wd_held, wide, mask_ref, bias_ref, copy_sem, send_sem, recv_sem,
):
    n_region, n_dev = shape
    region, dev = lax.axis_index("region"), lax.axis_index("dev")
    pairs = (
        (feat_hbm, feat),
        (occ_hbm, occ_ref),
        (w1_hbm, w_held.at[0]),
        (w2_hbm, w_held.at[1]),
        (wd_hbm, wd_held),
        (b1_hbm, b_held.at[0]),
        (b2_hbm, b_held.at[1]),
    )
    loads = [pltpu.make_async_copy(src, dst, copy_sem.at[k]) for k, (src, dst) in enumerate(pairs)]
    for load in loads:
        load.start()

    def there(dr, dd):
        r, d = region + dr, dev + dd
        return (r >= 0) & (r < n_region) & (d >= 0) & (d < n_dev)

    barrier = pltpu.get_barrier_semaphore()
    count = 0
    for dr, dd in CORNERS + FACES_X + FACES_Y:
        here = there(dr, dd)
        count = count + here.astype(jnp.int32)

        @pl.when(here)
        def _():
            pl.semaphore_signal(barrier, inc=1, device_id=(region + dr, dev + dd), device_id_type=MESH)

    made = []

    def transfer(dr, dd, src_x, dst_x):
        copy = pltpu.make_async_remote_copy(
            src_ref=grid.at[src_x, source_span(dd)],
            dst_ref=grid.at[dst_x, landing_span(dd)],
            send_sem=send_sem.at[len(made)],
            recv_sem=recv_sem.at[len(made)],
            device_id=(region + dr, dev + dd),
            device_id_type=MESH,
        )
        made.append((copy, there(dr, dd), there(-dr, -dd)))
        return made[-1]

    faces_x = [transfer(dr, dd, source_span(dr), landing_span(dr)) for dr, dd in FACES_X]
    low = [transfer(dr, dd, source_span(dr), landing_span(dr)) for dr, dd in CORNERS if dr > 0]
    chunks = []
    for x in range(H, H + E, CHUNK):
        chunks.append([transfer(dr, dd, pl.ds(x, CHUNK), pl.ds(x, CHUNK)) for dr, dd in FACES_Y])
    high = [transfer(dr, dd, source_span(dr), landing_span(dr)) for dr, dd in CORNERS if dr < 0]

    def arrived(group):
        for copy, _, comes in group:
            pl.when(comes)(copy.wait_recv)

    for dr, dd in CORNERS + FACES_X + FACES_Y:

        @pl.when(jnp.logical_not(there(-dr, -dd)))
        def _():
            nx, ny = (E if dr == 0 else H), (E if dd == 0 else H)
            grid[landing_span(dr), landing_span(dd)] = jnp.zeros((nx, ny, C, Z), jnp.bfloat16)

    loads[1].wait()
    bricks, devs = occ_ref.shape[1:]
    lanes = lax.broadcasted_iota(jnp.int32, (bricks, devs), 1)
    brick = lax.broadcasted_iota(jnp.int32, (bricks, Z), 0)
    voxel = lax.broadcasted_iota(jnp.int32, (bricks, Z), 1)
    span = Z // bricks
    inside = (voxel >= brick * span) & (voxel < (brick + 1) * span)
    for dr in (-1, 0, 1):
        valid = (region + dr >= 0) & (region + dr < n_region)
        held = occ_ref[jnp.clip(region + dr, 0, n_region - 1)].astype(jnp.float32)
        held = held * valid.astype(jnp.float32)
        for dd in (-1, 0, 1):
            level = jnp.sum(jnp.where(lanes == dev + dd, held, 0.0), axis=1, keepdims=True)
            mask_ref[dr + 1, dd + 1] = jnp.sum(jnp.where(inside, level, 0.0), axis=0, keepdims=True)

    mask = mask_ref[1, 1]
    loads[0].wait()
    for x in range(0, E, 2):
        slab = jnp.concatenate([feat[pl.ds(c * E * E + x * E, 2 * E), :] for c in range(C)], axis=0)
        blocks = jnp.swapaxes(slab.reshape(C, 2 * E, Z), 0, 1)
        blocks = jnp.where(mask[None] > 0, blocks, jnp.zeros_like(blocks))
        for k in range(2):
            grid[x + k + H, pl.ds(H, E)] = blocks[k * E : (k + 1) * E]

    pl.semaphore_wait(barrier, count)
    for group in [low] + chunks[:1] + [faces_x] + chunks[1:] + [high]:
        for copy, goes, _ in group:
            pl.when(goes)(copy.start)

    loads[2].wait()
    prepare_weight(w_held.at[0], w1)
    loads[3].wait()
    prepare_weight(w_held.at[1], w2)
    for k in range(2):
        loads[5 + k].wait()
        bias_ref[k] = jnp.broadcast_to(column(b_held[k]), (C, Z))
    loads[4].wait()
    wide[...] = wd_held[...].astype(jnp.float32)
    for c in range(2):
        for a in range(2):
            both = [wide[pl.ds(a * 4 + b * 2 + c, C, stride=8), :].astype(jnp.bfloat16) for b in range(2)]
            wd_ref[pl.ds(c * C, C), pl.ds(a * 2 * C, 2 * C)] = jnp.concatenate(both, axis=1)

    def side(at):
        return 0 if at == 0 else 2 if at == E + 1 else 1

    def put_first(x, y, value):
        first[x, y] = (value * mask_ref[side(x), side(y)]).astype(jnp.bfloat16)

    def put_second(x, y, value):
        second_ref[x, y] = (value * mask).astype(jnp.bfloat16)

    def one(x, y):
        conv_pair(grid, w1, bias_ref[0], ((x, y), (x, y + 1)), put_first)

    def two(x, y):
        conv_pair(first, w2, bias_ref[1], ((x, y), (x, y + 1)), put_second)

    for x in range(2, E):
        for y in range(2, E, 2):
            one(x, y)
    for x in range(2, E - 2):
        for y in range(2, E - 2, 2):
            two(x, y)
    arrived(faces_x)
    for x in (0, 1, E, E + 1):
        for y in range(2, E, 2):
            one(x, y)
    for x in (0, 1, E - 2, E - 1):
        for y in range(2, E - 2, 2):
            two(x, y)
    arrived(low)
    for k, group in enumerate(chunks + [high]):
        arrived(group)
        upto = H + CHUNK * (k + 1)
        for x in range(upto - CHUNK - 2, upto - 2):
            for y in (0, E):
                one(x, y)
        for x in range(max(upto - CHUNK - 4, 0), upto - 4):
            for y in (0, E - 2):
                two(x, y)
    for copy, goes, _ in made:
        pl.when(goes)(copy.wait_send)


def local_kernel(second_ref, wd_ref, bd_ref, skip_hbm, down_ref, slabs, narrow, copy_sem):
    copies = []
    for k, x in enumerate(range(0, E, 2)):
        slabs[k] = jnp.swapaxes(jnp.concatenate([second_ref[x], second_ref[x + 1]], axis=0), 0, 1)
        copy = pltpu.make_async_copy(slabs.at[k], skip_hbm.at[:, pl.ds(x * E, 2 * E), :], copy_sem.at[k])
        copy.start()
        copies.append(copy)

    lane_in = lax.broadcasted_iota(jnp.int32, (2 * Z, Z), 0)
    lane_out = lax.broadcasted_iota(jnp.int32, (2 * Z, Z), 1)
    keep = jnp.where(lane_in == 2 * lane_out, 1.0, 0.0).astype(jnp.bfloat16)
    bias = jnp.broadcast_to(column(bd_ref[...]), (C, 2 * Z))
    half = E // 2
    for x in range(half):
        for y in range(0, E, 4):
            stacked = [
                jnp.concatenate([second_ref[2 * x + a, y + 2 * k + b] for k in range(2)], axis=1)
                for a in range(2)
                for b in range(2)
            ]
            sums = jnp.dot(wd_ref[...], jnp.concatenate(stacked, axis=0), preferred_element_type=jnp.float32)
            moved = jnp.concatenate([pltpu.roll(sums[C:, k * Z : (k + 1) * Z], Z - 1, 1) for k in range(2)], axis=1)
            value = jnp.maximum(sums[:C] + moved + bias, 0.0).astype(jnp.bfloat16)
            narrow[y // 4, pl.ds(x, C, stride=half), :] = jnp.dot(value, keep, preferred_element_type=jnp.float32)
    for k in range(2):
        down_ref[:, :, pl.ds(k * Z, Z)] = narrow[k].reshape(C, half, Z).astype(jnp.bfloat16)
    for copy in copies:
        copy.wait()


def on_device(shape, features, occupancy, weight_one, bias_one, weight_two, bias_two, weight_down, bias_down):
    bf16, f32 = jnp.bfloat16, jnp.float32
    hbm = pl.BlockSpec(memory_space=pltpu.HBM)
    vmem = pl.BlockSpec(memory_space=pltpu.VMEM)
    rows = C * E * E
    held = [w.transpose(2, 3, 4, 0, 1).reshape(27, C, C) for w in (weight_one, weight_two)]
    n_copies = 6 + 2 * E // CHUNK
    operands = (
        features.reshape(rows, Z),
        occupancy.transpose(0, 2, 1),
        held[0],
        bias_one.reshape(1, C),
        held[1],
        bias_two.reshape(1, C),
        weight_down.transpose(0, 2, 3, 4, 1).reshape(8 * C, C),
    )
    second, wd = pl.pallas_call(
        functools.partial(remote_kernel, shape),
        out_shape=(jax.ShapeDtypeStruct((E, E, C, Z), bf16), jax.ShapeDtypeStruct((2 * C, 4 * C), bf16)),
        in_specs=[hbm] * len(operands),
        out_specs=(vmem, vmem),
        scratch_shapes=[
            pltpu.VMEM((rows, Z), bf16),
            pltpu.VMEM((shape[0], occupancy.shape[2], shape[1]), jnp.int32),
            pltpu.VMEM((2, 1, C), f32),
            pltpu.VMEM((E + 2 * H, E + 2 * H, C, Z), bf16),
            pltpu.VMEM((E + 2, E + 2, C, Z), bf16),
            pltpu.VMEM((2, 27, C, C), bf16),
            pltpu.VMEM((3 * C, TAPS * C), bf16),
            pltpu.VMEM((3 * C, TAPS * C), bf16),
            pltpu.VMEM((8 * C, C), bf16),
            pltpu.VMEM((8 * C, C), f32),
            pltpu.VMEM((3, 3, 1, Z), f32),
            pltpu.VMEM((2, C, Z), f32),
            pltpu.SemaphoreType.DMA((len(operands),)),
            pltpu.SemaphoreType.DMA((n_copies,)),
            pltpu.SemaphoreType.DMA((n_copies,)),
        ],
        compiler_params=pltpu.CompilerParams(
            collective_id=0, has_side_effects=True, vmem_limit_bytes=32 * 1024 * 1024
        ),
        name="halo_convs",
    )(*(pltpu.with_memory_space_constraint(operand, pltpu.HBM) for operand in operands))
    skip, down = pl.pallas_call(
        local_kernel,
        out_shape=(
            jax.ShapeDtypeStruct((C, E * E, Z), bf16),
            jax.ShapeDtypeStruct((C, E // 2, 2 * Z), bf16),
        ),
        in_specs=[vmem] * 3,
        out_specs=(hbm, vmem),
        scratch_shapes=[
            pltpu.VMEM((E // 2, C, 2 * E, Z), bf16),
            pltpu.VMEM((2, C * E // 2, Z), f32),
            pltpu.SemaphoreType.DMA((E // 2,)),
        ],
        compiler_params=pltpu.CompilerParams(vmem_limit_bytes=32 * 1024 * 1024),
        name="skip_and_down",
    )(second, wd, bias_down.reshape(1, C))
    return skip.reshape(C, E, E, Z), down


def solution(mesh):
    return jax.shard_map(
        functools.partial(on_device, (mesh.shape["region"], mesh.shape["dev"])),
        mesh=mesh,
        in_specs=(P(None, "region", "dev", None), P(), P(), P(), P(), P(), P(), P()),
        out_specs=(P(None, "region", "dev", None), P(None, "region", "dev")),
        check_vma=False,
    )
```

time: 25.1 us -> 22.3 us (0.89)
  the two profiles are of different devices: /device:TPU:121 before, /device:TPU:131 now
where the time goes in v3:
time: 22.3 us; the launch traced here: 22.2 us
  Pallas kernels  20.9 us (94%)
  local copies, waits for them, and re-layouts  0.65 us (3%)
  between operations  0.65 us (3%)
    pallas_call x1, Pallas kernels, on_device(): pl.pallas_call(functools.partial(remote_kernel, shape), out_shape=(jax.Sh...  17.8 us
    pallas_call x1, Pallas kernels, on_device(): pl.pallas_call(local_kernel, out_shape=(jax.ShapeDtypeStruct((C, E * E, Z...  3.17 us
    unnamed x2, local copies, waits for them, and re-layouts  0.65 us

profile of v3, /device:TPU:131, one launch (start us, length us, event | category | flops | bytes accessed | tf_op | source)
XLA Modules:
  0.0 22.2 jit_solution(9225851444084161587)
XLA Ops:
  0.6 17.8 %halo_convs.1 = (bf16[8,8,64,128]{3,2,1,0:T(8,128)(2,1)S(1)}, bf16[128,256]{1,0:T(8,128)(2,1)S(1)}) custom-call(bf16[4096,128]{1,0:T(8,128)(2,1)} %bitcast.16, s32[8,16,32]{2,1,0:T(8,128)} %bitcast.20, bf16[27,64,64]{2,1,0:T(8,128)(2,1)} %bitcast.17, f32[1,64]{1,0:T(1,128)} %bitcast.21, bf16[27,64,64]{2,1,0:T(8,128)(2,1)} %bitcast.18, f32[1,64]{1,0:T(1,128)} %bitcast.22, ...), custom_call_target="tpu_custom_call" | custom-call | tf_op jit(solution)/shard_map/halo_convs/pallas_call | solution.py:255
  18.4 0.0 copy-start
  18.4 0.6 %copy-done = f32[64]{0:T(128)S(1)} copy-done((f32[64]{0:T(128)S(1)}, f32[64]{0:T(128)}, u32[]{:S(2)}) %copy-start) | copy-done | bytes 280
  19.1 3.2 %skip_and_down.1 = (bf16[64,64,128]{2,1,0:T(8,128)(2,1)}, bf16[64,4,256]{2,1,0:T(4,128)(2,1)}) custom-call(bf16[8,8,64,128]{3,2,1,0:T(8,128)(2,1)S(1)} %get-tuple-element.6.second_ref, bf16[128,256]{1,0:T(8,128)(2,1)S(1)} %get-tuple-element.7.wd_ref, f32[1,64]{1,0:T(1,128)S(1)} %bitcast.15), custom_call_target="tpu_custom_call" | custom-call | tf_op jit(solution)/shard_map/skip_and_down/pallas_call | solution.py:282
Async XLA Ops:
  18.4 0.7 %copy-start = (f32[64]{0:T(128)S(1)}, f32[64]{0:T(128)}, u32[]{:S(2)}) copy-start(f32[64]{0:T(128)} %param.15) | copy-start | bytes 772

commit v4 on v3

v4 whole, which is shorter than its diff:
```python
import functools

import jax
import jax.numpy as jnp
from jax import lax
from jax.experimental import pallas as pl
from jax.experimental.pallas import tpu as pltpu
from jax.sharding import PartitionSpec as P

MESH = pl.DeviceIdType.MESH
FACES_X = ((1, 0), (-1, 0))
FACES_Y = ((0, 1), (0, -1))
CORNERS = ((1, 1), (1, -1), (-1, 1), (-1, -1))
DIRECT, PASSED = CORNERS[:2], CORNERS[2:]
E = 8
H = 2
C = 64
Z = 128
TAPS = 9
CHUNKS = ((0, 2), (2, 2), (4, 2), (6, 2))
SLABS = (0, 3, 1, 2)
SENDS = ("0", "near", "low", "far", "1", "2", "3")
TAKES = ("near", "0", "far", "low", "1", "2", "3", "high")


def source_span(step):
    return pl.ds(H, E) if step == 0 else pl.ds(E if step > 0 else H, H)


def landing_span(step):
    return pl.ds(H, E) if step == 0 else pl.ds(0 if step > 0 else E + H, H)


def column(row):
    spread = jnp.broadcast_to(row, (C, C))
    on_diagonal = lax.broadcasted_iota(jnp.int32, (C, C), 0) == lax.broadcasted_iota(jnp.int32, (C, C), 1)
    return jnp.sum(jnp.where(on_diagonal, spread, 0.0), axis=1, keepdims=True)


def prepare_weight(held, ready):
    for c in range(3):
        rows = pl.ds(c * C, C)
        for pair in range(TAPS // 2):
            both = jnp.concatenate([held[(2 * pair) * 3 + c], held[(2 * pair + 1) * 3 + c]], axis=1)
            ready[rows, pl.ds(pair * 2 * C, 2 * C)] = both
        ready[rows, pl.ds((TAPS - 1) * C, C)] = held[(TAPS - 1) * 3 + c]


def conv_pair(src, ready, bias, spots, put):
    stacked = []
    for a in range(3):
        for b in range(3):
            stacked.append(jnp.concatenate([src[x + a, y + b] for x, y in spots], axis=1))
    sums = jnp.dot(ready[...], jnp.concatenate(stacked, axis=0), preferred_element_type=jnp.float32)
    lane = lax.broadcasted_iota(jnp.int32, (C, Z), 1)
    for half, (x, y) in enumerate(spots):
        part = sums[:, half * Z : (half + 1) * Z]
        before = jnp.where(lane == 0, 0.0, pltpu.roll(part[:C], 1, 1))
        after = jnp.where(lane == Z - 1, 0.0, pltpu.roll(part[2 * C :], Z - 1, 1))
        put(x, y, jnp.maximum(part[C : 2 * C] + before + after + bias, 0.0))


def remote_kernel(
    shape, feat_hbm, occ_hbm, w1_hbm, b1_hbm, w2_hbm, b2_hbm, wd_hbm, bd_hbm, slab_ref, down_ref,
    feat, occ_ref, b_held, grid, first, second, w_held, w1, w2, wd_held, wide, wd, keep, narrow, mask_ref, bias_ref,
    copy_sem, send_sem, recv_sem,
):
    n_region, n_dev = shape
    region, dev = lax.axis_index("region"), lax.axis_index("dev")
    pairs = (
        (occ_hbm, occ_ref),
        (w1_hbm, w_held.at[0]),
        (w2_hbm, w_held.at[1]),
        (wd_hbm, wd_held),
        (b1_hbm, b_held.at[0]),
        (b2_hbm, b_held.at[1]),
        (bd_hbm, b_held.at[2]),
    )
    planes = []
    for k in range(E // 2):
        part = feat_hbm.at[:, pl.ds(2 * k * E, 2 * E), :]
        planes.append(pltpu.make_async_copy(part, feat.at[k], copy_sem.at[len(pairs) + k]))
    loads = [pltpu.make_async_copy(src, dst, copy_sem.at[k]) for k, (src, dst) in enumerate(pairs)]
    loads[0].start()
    for k in SLABS:
        planes[k].start()
    for load in loads[1:]:
        load.start()

    def there(dr, dd):
        r, d = region + dr, dev + dd
        return (r >= 0) & (r < n_region) & (d >= 0) & (d < n_dev)

    barrier = pltpu.get_barrier_semaphore()
    count = 0
    for dr, dd in FACES_Y + FACES_X + DIRECT:
        count = count + there(dr, dd).astype(jnp.int32)

        @pl.when(there(-dr, -dd))
        def _():
            pl.semaphore_signal(barrier, inc=1, device_id=(region - dr, dev - dd), device_id_type=MESH)

    made = []

    def transfer(to, src, dst, goes, comes):
        copy = pltpu.make_async_remote_copy(
            src_ref=grid.at[src],
            dst_ref=grid.at[dst],
            send_sem=send_sem.at[len(made)],
            recv_sem=recv_sem.at[len(made)],
            device_id=(region + to[0], dev + to[1]),
            device_id_type=MESH,
        )
        made.append((copy, goes, comes))
        return made[-1]

    def straight(dr, dd):
        src, dst = (source_span(dr), source_span(dd)), (landing_span(dr), landing_span(dd))
        return transfer((dr, dd), src, dst, there(dr, dd), there(-dr, -dd))

    def passed_on(dr, dd):
        src, dst = (source_span(dr), landing_span(dd)), (landing_span(dr), landing_span(dd))
        return transfer((dr, 0), src, dst, there(dr, 0) & there(dr, -dd) & there(0, -dd), there(-dr, -dd))

    groups = {"low": [straight(*way) for way in DIRECT], "high": [passed_on(*way) for way in PASSED]}
    for name, up, down in (("near", (E + 1, 1), (H, E + H)), ("far", (E, 0), (H + 1, E + H + 1))):
        groups[name] = []
        for dr, (src, dst) in ((1, up), (-1, down)):
            src, dst = (pl.ds(src, 1), pl.ds(H, E)), (pl.ds(dst, 1), pl.ds(H, E))
            groups[name].append(transfer((dr, 0), src, dst, there(dr, 0), there(-dr, 0)))
    for k, (first_x, planes_x) in enumerate(CHUNKS):
        groups[str(k)] = []
        x = pl.ds(H + first_x, planes_x)
        for dr, dd in FACES_Y:
            src, dst = (x, source_span(dd)), (x, landing_span(dd))
            groups[str(k)].append(transfer((dr, dd), src, dst, there(dr, dd), there(-dr, -dd)))

    def start(group):
        for copy, goes, _ in group:
            pl.when(goes)(copy.start)

    def arrived(group):
        for copy, _, comes in group:
            pl.when(comes)(copy.wait_recv)

    loads[0].wait()
    bricks, devs = occ_ref.shape[1:]
    lanes = lax.broadcasted_iota(jnp.int32, (bricks, devs), 1)
    brick = lax.broadcasted_iota(jnp.int32, (bricks, Z), 0)
    voxel = lax.broadcasted_iota(jnp.int32, (bricks, Z), 1)
    span = Z // bricks
    inside = (voxel >= brick * span) & (voxel < (brick + 1) * span)
    for dr in (-1, 0, 1):
        valid = (region + dr >= 0) & (region + dr < n_region)
        held = occ_ref[jnp.clip(region + dr, 0, n_region - 1)].astype(jnp.float32)
        held = held * valid.astype(jnp.float32)
        for dd in (-1, 0, 1):
            level = jnp.sum(jnp.where(lanes == dev + dd, held, 0.0), axis=1, keepdims=True)
            mask_ref[dr + 1, dd + 1] = jnp.sum(jnp.where(inside, level, 0.0), axis=0, keepdims=True)

    mask = mask_ref[1, 1]
    for k in SLABS:
        planes[k].wait()
        blocks = jnp.swapaxes(feat[k], 0, 1)
        blocks = jnp.where(mask[None] > 0, blocks, jnp.zeros_like(blocks))
        for h in range(2):
            grid[2 * k + h + H, pl.ds(H, E)] = blocks[h * E : (h + 1) * E]

    def side(at):
        return 0 if at == 0 else 2 if at == E + 1 else 1

    def put_first(x, y, value):
        first[x, y] = (value * mask_ref[side(x), side(y)]).astype(jnp.bfloat16)

    def put_second(x, y, value):
        second[x, y] = (value * mask).astype(jnp.bfloat16)

    def one(x, y):
        conv_pair(grid, w1, bias_ref[0], ((x, y), (x, y + 1)), put_first)

    def two(x, y):
        conv_pair(first, w2, bias_ref[1], ((x, y), (x, y + 1)), put_second)

    def finish(k):
        x = 2 * k
        slab_ref[k] = jnp.swapaxes(jnp.concatenate([second[x], second[x + 1]], axis=0), 0, 1)
        stacked = []
        for a in range(2):
            for b in range(2):
                stacked.append(jnp.concatenate([second[x + a, y + b] for y in range(0, E, 2)], axis=1))
        sums = jnp.dot(wd[...], jnp.concatenate(stacked, axis=0), preferred_element_type=jnp.float32)
        lowered = []
        for y in range(E // 2):
            part = sums[:, y * Z : (y + 1) * Z]
            value = part[:C] + pltpu.roll(part[C:], Z - 1, 1) + bias_ref[2]
            lowered.append(jnp.maximum(value, 0.0).astype(jnp.bfloat16))
        for h in range(2):
            both = jnp.concatenate(lowered[2 * h : 2 * h + 2], axis=1)
            kept = jnp.dot(both, keep[...], preferred_element_type=jnp.float32)
            narrow[h, pl.ds(k, C, stride=E // 2), :] = kept

    pl.semaphore_wait(barrier, count)
    for name in SENDS:
        start(groups[name])

    for dr, dd in CORNERS + FACES_X + FACES_Y:

        @pl.when(jnp.logical_not(there(-dr, -dd)))
        def _():
            nx, ny = (E if dr == 0 else H), (E if dd == 0 else H)
            grid[landing_span(dr), landing_span(dd)] = jnp.zeros((nx, ny, C, Z), jnp.bfloat16)

    loads[1].wait()
    prepare_weight(w_held.at[0], w1)
    for k in range(3):
        loads[4 + k].wait()
        bias_ref[k] = jnp.broadcast_to(column(b_held[k]), (C, Z))
    for x in range(2, E):
        for y in range(2, E, 2):
            one(x, y)
    loads[2].wait()
    prepare_weight(w_held.at[1], w2)
    loads[3].wait()
    wide[...] = wd_held[...].astype(jnp.float32)
    for c in range(2):
        for a in range(2):
            both = [wide[pl.ds(a * 4 + b * 2 + c, C, stride=8), :].astype(jnp.bfloat16) for b in range(2)]
            wd[pl.ds(c * C, C), pl.ds(a * 2 * C, 2 * C)] = jnp.concatenate(both, axis=1)
    lane_in = lax.broadcasted_iota(jnp.int32, (2 * Z, Z), 0)
    lane_out = lax.broadcasted_iota(jnp.int32, (2 * Z, Z), 1)
    keep[...] = jnp.where(lane_in == 2 * lane_out, 1.0, 0.0).astype(jnp.bfloat16)

    for x in range(2, E - 2):
        for y in range(2, E - 2, 2):
            two(x, y)

    landed, landed_rim = set(range(H, E + H)), set()
    one_middle, one_rim = set(range(2, E)), set()
    two_middle, two_rim = set(range(2, E - 2)), set()

    def advance():
        for x in range(E + 2):
            if x not in one_middle and {x, x + 1, x + 2} <= landed:
                for y in range(2, E, 2):
                    one(x, y)
                one_middle.add(x)
        for x in range(E):
            if x not in two_middle and {x, x + 1, x + 2} <= one_middle:
                for y in range(2, E - 2, 2):
                    two(x, y)
                two_middle.add(x)
        for x in range(E + 2):
            if x not in one_rim and {x, x + 1, x + 2} <= landed_rim:
                for y in (0, E):
                    one(x, y)
                one_rim.add(x)
        for x in range(E):
            if x not in two_rim and {x, x + 1, x + 2} <= one_rim & one_middle:
                for y in (0, E - 2):
                    two(x, y)
                two_rim.add(x)
                if x ^ 1 in two_rim:
                    finish(x // 2)

    for name in TAKES:
        arrived(groups[name])
        if name == "near":
            landed.update((1, E + H))
        elif name == "far":
            landed.update((0, E + H + 1))
        elif name == "low":
            landed_rim.update(range(H))
        elif name == "high":
            landed_rim.update(range(E + H, E + 2 * H))
        else:
            first_x, planes_x = CHUNKS[int(name)]
            landed_rim.update(range(H + first_x, H + first_x + planes_x))
            if first_x == 0:
                start(groups["high"])
        advance()
    for k in range(2):
        down_ref[:, :, pl.ds(k * Z, Z)] = narrow[k].reshape(C, E // 2, Z).astype(jnp.bfloat16)
    for copy, goes, _ in made:
        pl.when(goes)(copy.wait_send)


def local_kernel(slab_ref, down_in, skip_hbm, down_hbm, copy_sem):
    copies = [pltpu.make_async_copy(down_in, down_hbm, copy_sem.at[E // 2])]
    for k in range(E // 2):
        copies.append(pltpu.make_async_copy(slab_ref.at[k], skip_hbm.at[:, pl.ds(2 * k * E, 2 * E), :], copy_sem.at[k]))
    for copy in copies:
        copy.start()
    for copy in copies:
        copy.wait()


def on_device(shape, features, occupancy, weight_one, bias_one, weight_two, bias_two, weight_down, bias_down):
    bf16, f32 = jnp.bfloat16, jnp.float32
    hbm = pl.BlockSpec(memory_space=pltpu.HBM)
    vmem = pl.BlockSpec(memory_space=pltpu.VMEM)
    held = [w.transpose(2, 3, 4, 0, 1).reshape(27, C, C) for w in (weight_one, weight_two)]
    n_copies = 2 * len(CHUNKS) + 8
    n_loads = 7 + E // 2
    operands = (
        features.reshape(C, E * E, Z),
        occupancy.transpose(0, 2, 1),
        held[0],
        bias_one.reshape(1, C),
        held[1],
        bias_two.reshape(1, C),
        weight_down.transpose(0, 2, 3, 4, 1).reshape(8 * C, C),
        bias_down.reshape(1, C),
    )
    slabs, down = pl.pallas_call(
        functools.partial(remote_kernel, shape),
        out_shape=(
            jax.ShapeDtypeStruct((E // 2, C, 2 * E, Z), bf16),
            jax.ShapeDtypeStruct((C, E // 2, 2 * Z), bf16),
        ),
        in_specs=[hbm] * len(operands),
        out_specs=(vmem, vmem),
        scratch_shapes=[
            pltpu.VMEM((E // 2, C, 2 * E, Z), bf16),
            pltpu.VMEM((shape[0], occupancy.shape[2], shape[1]), jnp.int32),
            pltpu.VMEM((3, 1, C), f32),
            pltpu.VMEM((E + 2 * H, E + 2 * H, C, Z), bf16),
            pltpu.VMEM((E + 2, E + 2, C, Z), bf16),
            pltpu.VMEM((E, E, C, Z), bf16),
            pltpu.VMEM((2, 27, C, C), bf16),
            pltpu.VMEM((3 * C, TAPS * C), bf16),
            pltpu.VMEM((3 * C, TAPS * C), bf16),
            pltpu.VMEM((8 * C, C), bf16),
            pltpu.VMEM((8 * C, C), f32),
            pltpu.VMEM((2 * C, 4 * C), bf16),
            pltpu.VMEM((2 * Z, Z), bf16),
            pltpu.VMEM((2, C * E // 2, Z), f32),
            pltpu.VMEM((3, 3, 1, Z), f32),
            pltpu.VMEM((3, C, Z), f32),
            pltpu.SemaphoreType.DMA((n_loads,)),
            pltpu.SemaphoreType.DMA((n_copies,)),
            pltpu.SemaphoreType.DMA((n_copies,)),
        ],
        compiler_params=pltpu.CompilerParams(
            collective_id=0, has_side_effects=True, vmem_limit_bytes=32 * 1024 * 1024
        ),
        name="halo_convs",
    )(*(pltpu.with_memory_space_constraint(operand, pltpu.HBM) for operand in operands))
    skip, down = pl.pallas_call(
        local_kernel,
        out_shape=(
            jax.ShapeDtypeStruct((C, E * E, Z), bf16),
            jax.ShapeDtypeStruct((C, E // 2, 2 * Z), bf16),
        ),
        in_specs=[vmem] * 2,
        out_specs=(hbm, hbm),
        scratch_shapes=[pltpu.SemaphoreType.DMA((E // 2 + 1,))],
        compiler_params=pltpu.CompilerParams(vmem_limit_bytes=32 * 1024 * 1024),
        name="copy_out",
    )(slabs, down)
    return skip.reshape(C, E, E, Z), down


def solution(mesh):
    return jax.shard_map(
        functools.partial(on_device, (mesh.shape["region"], mesh.shape["dev"])),
        mesh=mesh,
        in_specs=(P(None, "region", "dev", None), P(), P(), P(), P(), P(), P(), P()),
        out_specs=(P(None, "region", "dev", None), P(None, "region", "dev")),
        check_vma=False,
    )
```

time: 22.3 us -> 19.6 us (0.88)
  the two profiles are of different devices: /device:TPU:131 before, /device:TPU:121 now
where the time goes in v4:
time: 19.6 us; the launch traced here: 19.4 us
  Pallas kernels  18.8 us (96%)
  between operations  0.64 us (3%)
    pallas_call x1, Pallas kernels, on_device(): pl.pallas_call(functools.partial(remote_kernel, shape), out_shape=(jax.Sh...  17.7 us
    pallas_call x1, Pallas kernels, on_device(): pl.pallas_call(local_kernel, out_shape=(jax.ShapeDtypeStruct((C, E * E, Z...  1.05 us

profile of v4, /device:TPU:121, one launch (start us, length us, event | category | flops | bytes accessed | tf_op | source)
XLA Modules:
  0.0 19.4 jit_solution(8375693179385285237)
XLA Ops:
  0.6 17.7 %halo_convs.1 = (bf16[4,64,16,128]{3,2,1,0:T(8,128)(2,1)S(1)}, bf16[64,4,256]{2,1,0:T(4,128)(2,1)S(1)}) custom-call(bf16[64,64,128]{2,1,0:T(8,128)(2,1)} %bitcast.15, s32[8,16,32]{2,1,0:T(8,128)} %bitcast.19, bf16[27,64,64]{2,1,0:T(8,128)(2,1)} %bitcast.16, f32[1,64]{1,0:T(1,128)} %bitcast.20, bf16[27,64,64]{2,1,0:T(8,128)(2,1)} %bitcast.17, ...), custom_call_target="tpu_custom_call" | custom-call | tf_op jit(solution)/shard_map/halo_convs/pallas_call | solution.py:314
  18.3 1.0 %copy_out.1 = (bf16[64,64,128]{2,1,0:T(8,128)(2,1)}, bf16[64,4,256]{2,1,0:T(4,128)(2,1)}) custom-call(bf16[4,64,16,128]{3,2,1,0:T(8,128)(2,1)S(1)} %get-tuple-element.6.slab_ref, bf16[64,4,256]{2,1,0:T(4,128)(2,1)S(1)} %get-tuple-element.7.down_in), custom_call_target="tpu_custom_call" | custom-call | tf_op jit(solution)/shard_map/copy_out/pallas_call | solution.py:348

commit v5 on v4

--- a/solution.py
+++ b/solution.py
@@ -20,7 +20,7 @@
 CHUNKS = ((0, 2), (2, 2), (4, 2), (6, 2))
 SLABS = (0, 3, 1, 2)
 SENDS = ("0", "near", "low", "far", "1", "2", "3")
-TAKES = ("near", "0", "far", "low", "1", "2", "3", "high")
+TAKES = ("0", "near", "far", "low", "1", "2", "3", "high")
 
 
 def source_span(step):
@@ -181,7 +181,7 @@
     def two(x, y):
         conv_pair(first, w2, bias_ref[1], ((x, y), (x, y + 1)), put_second)
 
-    def finish(k):
+    def lower(k):
         x = 2 * k
         slab_ref[k] = jnp.swapaxes(jnp.concatenate([second[x], second[x + 1]], axis=0), 0, 1)
         stacked = []
@@ -194,6 +194,9 @@
             part = sums[:, y * Z : (y + 1) * Z]
             value = part[:C] + pltpu.roll(part[C:], Z - 1, 1) + bias_ref[2]
             lowered.append(jnp.maximum(value, 0.0).astype(jnp.bfloat16))
+        return lowered
+
+    def thin(k, lowered):
         for h in range(2):
             both = jnp.concatenate(lowered[2 * h : 2 * h + 2], axis=1)
             kept = jnp.dot(both, keep[...], preferred_element_type=jnp.float32)
@@ -238,29 +241,38 @@
     one_middle, one_rim = set(range(2, E)), set()
     two_middle, two_rim = set(range(2, E - 2)), set()
 
-    def advance():
+    complete = []
+
+    def advance(last):
+        lowered = [(k, lower(k)) for k in complete]
+        complete.clear()
         for x in range(E + 2):
             if x not in one_middle and {x, x + 1, x + 2} <= landed:
                 for y in range(2, E, 2):
                     one(x, y)
                 one_middle.add(x)
+        for x in range(E + 2):
+            if x not in one_rim and {x, x + 1, x + 2} <= landed_rim:
+                for y in (0, E):
+                    one(x, y)
+                one_rim.add(x)
+        for k, planes_k in lowered:
+            thin(k, planes_k)
         for x in range(E):
             if x not in two_middle and {x, x + 1, x + 2} <= one_middle:
                 for y in range(2, E - 2, 2):
                     two(x, y)
                 two_middle.add(x)
-        for x in range(E + 2):
-            if x not in one_rim and {x, x + 1, x + 2} <= landed_rim:
-                for y in (0, E):
-                    one(x, y)
-                one_rim.add(x)
         for x in range(E):
             if x not in two_rim and {x, x + 1, x + 2} <= one_rim & one_middle:
                 for y in (0, E - 2):
                     two(x, y)
                 two_rim.add(x)
                 if x ^ 1 in two_rim:
-                    finish(x // 2)
+                    complete.append(x // 2)
+        if last:
+            for k, planes_k in [(k, lower(k)) for k in complete]:
+                thin(k, planes_k)
 
     for name in TAKES:
         arrived(groups[name])
@@ -277,7 +289,8 @@
             landed_rim.update(range(H + first_x, H + first_x + planes_x))
             if first_x == 0:
                 start(groups["high"])
-        advance()
+        if name != "3":
+            advance(name == TAKES[-1])
     for k in range(2):
         down_ref[:, :, pl.ds(k * Z, Z)] = narrow[k].reshape(C, E // 2, Z).astype(jnp.bfloat16)
     for copy, goes, _ in made:

time: 19.6 us -> 18.6 us (0.949)
  Pallas kernels: 18.8 us -> 17.9 us
    pallas_call x1, Pallas kernels: 17.7 us -> 16.8 us  [on_device(): pl.pallas_call(functools.partial(remote_kernel, shape), out_shape=(jax.Sh...]
where the time goes in v5:
time: 18.6 us; the launch traced here: 18.5 us
  Pallas kernels  17.9 us (96%)
  between operations  0.64 us (3%)
    pallas_call x1, Pallas kernels, on_device(): pl.pallas_call(functools.partial(remote_kernel, shape), out_shape=(jax.Sh...  16.8 us
    pallas_call x1, Pallas kernels, on_device(): pl.pallas_call(local_kernel, out_shape=(jax.ShapeDtypeStruct((C, E * E, Z...  1.05 us

profile of v5, /device:TPU:121, one launch (start us, length us, event | category | flops | bytes accessed | tf_op | source)
XLA Modules:
  0.0 18.5 jit_solution(11291969132246090119)
XLA Ops:
  0.6 16.8 %halo_convs.1 = (bf16[4,64,16,128]{3,2,1,0:T(8,128)(2,1)S(1)}, bf16[64,4,256]{2,1,0:T(4,128)(2,1)S(1)}) custom-call(bf16[64,64,128]{2,1,0:T(8,128)(2,1)} %bitcast.15, s32[8,16,32]{2,1,0:T(8,128)} %bitcast.19, bf16[27,64,64]{2,1,0:T(8,128)(2,1)} %bitcast.16, f32[1,64]{1,0:T(1,128)} %bitcast.20, bf16[27,64,64]{2,1,0:T(8,128)(2,1)} %bitcast.17, ...), custom_call_target="tpu_custom_call" | custom-call | tf_op jit(solution)/shard_map/halo_convs/pallas_call | solution.py:327
  17.5 1.0 %copy_out.1 = (bf16[64,64,128]{2,1,0:T(8,128)(2,1)}, bf16[64,4,256]{2,1,0:T(4,128)(2,1)}) custom-call(bf16[4,64,16,128]{3,2,1,0:T(8,128)(2,1)S(1)} %get-tuple-element.6.slab_ref, bf16[64,4,256]{2,1,0:T(4,128)(2,1)S(1)} %get-tuple-element.7.down_in), custom_call_target="tpu_custom_call" | custom-call | tf_op jit(solution)/shard_map/copy_out/pallas_call | solution.py:361

commit v6 on v5

--- a/solution.py
+++ b/solution.py
@@ -196,11 +196,18 @@
             lowered.append(jnp.maximum(value, 0.0).astype(jnp.bfloat16))
         return lowered
 
-    def thin(k, lowered):
-        for h in range(2):
-            both = jnp.concatenate(lowered[2 * h : 2 * h + 2], axis=1)
-            kept = jnp.dot(both, keep[...], preferred_element_type=jnp.float32)
-            narrow[h, pl.ds(k, C, stride=E // 2), :] = kept
+    def thin(planes):
+        rows = []
+        for _, lowered in planes:
+            for h in range(2):
+                rows.append(jnp.concatenate(lowered[2 * h : 2 * h + 2], axis=1))
+        if not rows:
+            return
+        kept = jnp.dot(jnp.concatenate(rows, axis=0), keep[...], preferred_element_type=jnp.float32)
+        for i, (k, _) in enumerate(planes):
+            for h in range(2):
+                at = (2 * i + h) * C
+                narrow[h, pl.ds(k, C, stride=E // 2), :] = kept[at : at + C]
 
     pl.semaphore_wait(barrier, count)
     for name in SENDS:
@@ -256,8 +263,7 @@
                 for y in (0, E):
                     one(x, y)
                 one_rim.add(x)
-        for k, planes_k in lowered:
-            thin(k, planes_k)
+        thin(lowered)
         for x in range(E):
             if x not in two_middle and {x, x + 1, x + 2} <= one_middle:
                 for y in range(2, E - 2, 2):
@@ -271,8 +277,7 @@
                 if x ^ 1 in two_rim:
                     complete.append(x // 2)
         if last:
-            for k, planes_k in [(k, lower(k)) for k in complete]:
-                thin(k, planes_k)
+            thin([(k, lower(k)) for k in complete])
 
     for name in TAKES:
         arrived(groups[name])

time: 18.6 us -> 18.5 us (level)
  Pallas kernels: 17.9 us -> 17.7 us
where the time goes in v6:
time: 18.5 us; the launch traced here: 18.4 us
  Pallas kernels  17.7 us (96%)
  between operations  0.64 us (3%)
    pallas_call x1, Pallas kernels, on_device(): pl.pallas_call(functools.partial(remote_kernel, shape), out_shape=(jax.Sh...  16.7 us
    pallas_call x1, Pallas kernels, on_device(): pl.pallas_call(local_kernel, out_shape=(jax.ShapeDtypeStruct((C, E * E, Z...  1.05 us

profile of v6, /device:TPU:121, one launch (start us, length us, event | category | flops | bytes accessed | tf_op | source)
XLA Modules:
  0.0 18.4 jit_solution(13705271137813165739)
XLA Ops:
  0.6 16.7 %halo_convs.1 = (bf16[4,64,16,128]{3,2,1,0:T(8,128)(2,1)S(1)}, bf16[64,4,256]{2,1,0:T(4,128)(2,1)S(1)}) custom-call(bf16[64,64,128]{2,1,0:T(8,128)(2,1)} %bitcast.15, s32[8,16,32]{2,1,0:T(8,128)} %bitcast.19, bf16[27,64,64]{2,1,0:T(8,128)(2,1)} %bitcast.16, f32[1,64]{1,0:T(1,128)} %bitcast.20, bf16[27,64,64]{2,1,0:T(8,128)(2,1)} %bitcast.17, ...), custom_call_target="tpu_custom_call" | custom-call | tf_op jit(solution)/shard_map/halo_convs/pallas_call | solution.py:332
  17.3 1.0 %copy_out.1 = (bf16[64,64,128]{2,1,0:T(8,128)(2,1)}, bf16[64,4,256]{2,1,0:T(4,128)(2,1)}) custom-call(bf16[4,64,16,128]{3,2,1,0:T(8,128)(2,1)S(1)} %get-tuple-element.6.slab_ref, bf16[64,4,256]{2,1,0:T(4,128)(2,1)S(1)} %get-tuple-element.7.down_in), custom_call_target="tpu_custom_call" | custom-call | tf_op jit(solution)/shard_map/copy_out/pallas_call | solution.py:366

commit v7 on v6

--- a/solution.py
+++ b/solution.py
@@ -231,7 +231,7 @@
     loads[2].wait()
     prepare_weight(w_held.at[1], w2)
     loads[3].wait()
-    wide[...] = wd_held[...].astype(jnp.float32)
+    wide[pl.ds(0, 8 * C), :] = wd_held[...].astype(jnp.float32)
     for c in range(2):
         for a in range(2):
             both = [wide[pl.ds(a * 4 + b * 2 + c, C, stride=8), :].astype(jnp.bfloat16) for b in range(2)]
@@ -297,7 +297,7 @@
         if name != "3":
             advance(name == TAKES[-1])
     for k in range(2):
-        down_ref[:, :, pl.ds(k * Z, Z)] = narrow[k].reshape(C, E // 2, Z).astype(jnp.bfloat16)
+        down_ref[:, :, pl.ds(k * Z, Z)] = narrow[k, pl.ds(0, C * E // 2), :].reshape(C, E // 2, Z).astype(jnp.bfloat16)
     for copy, goes, _ in made:
         pl.when(goes)(copy.wait_send)
 
@@ -348,10 +348,10 @@
             pltpu.VMEM((3 * C, TAPS * C), bf16),
             pltpu.VMEM((3 * C, TAPS * C), bf16),
             pltpu.VMEM((8 * C, C), bf16),
-            pltpu.VMEM((8 * C, C), f32),
+            pltpu.VMEM((8 * C + 8, C), f32),
             pltpu.VMEM((2 * C, 4 * C), bf16),
             pltpu.VMEM((2 * Z, Z), bf16),
-            pltpu.VMEM((2, C * E // 2, Z), f32),
+            pltpu.VMEM((2, C * E // 2 + 8, Z), f32),
             pltpu.VMEM((3, 3, 1, Z), f32),
             pltpu.VMEM((3, C, Z), f32),
             pltpu.SemaphoreType.DMA((n_loads,)),

time: 18.5 us -> 18.5 us (level)
  no operation moved by 1% of the time
where the time goes in v7:
time: 18.5 us; the launch traced here: 18.4 us
  Pallas kernels  17.7 us (96%)
  between operations  0.64 us (3%)
    pallas_call x1, Pallas kernels, on_device(): pl.pallas_call(functools.partial(remote_kernel, shape), out_shape=(jax.Sh...  16.7 us
    pallas_call x1, Pallas kernels, on_device(): pl.pallas_call(local_kernel, out_shape=(jax.ShapeDtypeStruct((C, E * E, Z...  1.05 us

profile of v7, /device:TPU:121, one launch (start us, length us, event | category | flops | bytes accessed | tf_op | source)
XLA Modules:
  0.0 18.4 jit_solution(3658621175267613856)
XLA Ops:
  0.6 16.7 %halo_convs.1 = (bf16[4,64,16,128]{3,2,1,0:T(8,128)(2,1)S(1)}, bf16[64,4,256]{2,1,0:T(4,128)(2,1)S(1)}) custom-call(bf16[64,64,128]{2,1,0:T(8,128)(2,1)} %bitcast.15, s32[8,16,32]{2,1,0:T(8,128)} %bitcast.19, bf16[27,64,64]{2,1,0:T(8,128)(2,1)} %bitcast.16, f32[1,64]{1,0:T(1,128)} %bitcast.20, bf16[27,64,64]{2,1,0:T(8,128)(2,1)} %bitcast.17, ...), custom_call_target="tpu_custom_call" | custom-call | tf_op jit(solution)/shard_map/halo_convs/pallas_call | solution.py:332
  17.3 1.0 %copy_out.1 = (bf16[64,64,128]{2,1,0:T(8,128)(2,1)}, bf16[64,4,256]{2,1,0:T(4,128)(2,1)}) custom-call(bf16[4,64,16,128]{3,2,1,0:T(8,128)(2,1)S(1)} %get-tuple-element.6.slab_ref, bf16[64,4,256]{2,1,0:T(4,128)(2,1)S(1)} %get-tuple-element.7.down_in), custom_call_target="tpu_custom_call" | custom-call | tf_op jit(solution)/shard_map/copy_out/pallas_call | solution.py:366
